TPU v7x, 32 devices: a whole 2x2x4 slice. The times are simulated.
32 devices in a mesh: lon: 8 (over z, core), lat: 4 (over y, x).
Axes of the slice: x: 2, y: 2, z: 4, core: 2. Of those that a mesh axis runs over, the one named last changes fastest.
Arguments:
- adjoint_height: float32 [2048, 1024], P('lat', 'lon'), may hold values from -6 to 6
- depth: float32 [2048, 1024], P('lat', 'lon'), may hold values from 0.1 to 1
- wet: int32 [2048, 1024], P('lat', 'lon'), may hold values 0 or 1
- basis_lat: float32 [32, 2048], P(None, 'lat'), may hold values from -1.5 to 1.5
- basis_lon: float32 [32, 1024], P(None, 'lon'), may hold values from -1.5 to 1.5
- tile_owner: int32 [128, 64], P('lat', 'lon'), may hold values from 0 to 7, as said below
- tile_patch: int32 [128, 64], P('lat', 'lon'), may hold values from 0 to 255
- tile_count: int32 [128, 64], P('lat', 'lon'), may hold values from 1 to 32
- prior_patches: float32 [4, 8, 256, 256], P('lat', 'lon'), may hold values from 0 to 11
- prior_subfaults: float32 [32, 32], replicated, may hold values from -0.4 to 1.7
Outputs:
- adjoint_final: float32 [2048, 1024], P('lat', 'lon')
- source_gradient: float32 [2048, 1024], P('lat', 'lon')
Inputs may be any that keep to these rules, and one draw needn't show every extreme that they name: `tile_owner`: within each device's block of tiles no owner is named more than 56 times, and in every latitude band one owner is named exactly 56 times by every device's block.
All inputs are finite; a program needn't handle non-finite values. No bound on the sum of `wet` on one device may be relied on, other than what follows from the above.
Results may differ from a plain program's by a relative error of at most 0.0002.
Values sent between devices are 32-bit elements; how exact they have to be, the bound alone decides.
A program may use at most 64 MiB of HBM per device.

v0:
```python
import jax
import jax.numpy as jnp
from jax import lax
from jax.sharding import PartitionSpec as P

STEPS = 4
TS = 16
SUB = 32
NPATCH = 256


COURANT = 0.6


def padded(block, sides, width, periodic):
    for axis, dim in sides:
        count = lax.axis_size(axis)
        forward = [(i, i + 1) for i in range(count - 1)]
        if periodic:
            forward.append((count - 1, 0))
        backward = [(target, source) for source, target in forward]
        low = lax.ppermute(
            lax.slice_in_dim(block, block.shape[dim] - width, None, axis=dim), axis, forward
        )
        high = lax.ppermute(lax.slice_in_dim(block, 0, width, axis=dim), axis, backward)
        block = jnp.concatenate([low, block, high], axis=dim)
    return block


def adjoint_step(height, east, north, wet_depth):
    east_new = east[:, :-1] + COURANT * jnp.minimum(wet_depth[:, :-1], wet_depth[:, 1:]) * (
        height[:, 1:] - height[:, :-1]
    )
    north_new = north[:-1, :] + COURANT * jnp.minimum(wet_depth[:-1, :], wet_depth[1:, :]) * (
        height[1:, :] - height[:-1, :]
    )
    height_new = (
        height[1:-1, 1:-1]
        + COURANT * (east_new[1:-1, 1:] - east_new[1:-1, :-1])
        + COURANT * (north_new[1:, 1:-1] - north_new[:-1, 1:-1])
    )
    return (height_new, east_new[1:-1, 1:], north_new[1:, 1:-1])


def widen(fields, rim_width):
    looped = padded(fields, (("lon", 2),), rim_width, True)
    return padded(looped, (("lat", 1),), rim_width, False)


def local(
    adjoint_height,
    depth,
    wet,
    basis_lat,
    basis_lon,
    tile_owner,
    tile_patch,
    tile_count,
    prior_patches,
    prior_subfaults,
):
    highest = lax.Precision.HIGHEST
    lat_cells, lon_cells = adjoint_height.shape
    wet_depth = depth * wet.astype(jnp.float32)
    opening = widen(jnp.stack([adjoint_height, wet_depth]), 1)
    depth_rim = opening[1]
    blank = jnp.zeros_like(opening[0])
    height, east, north = adjoint_step(opening[0], blank, blank, depth_rim)
    for repeat in range(1, STEPS):
        widened = widen(jnp.stack([height, east, north]), 1)
        height, east, north = adjoint_step(widened[0], widened[1], widened[2], depth_rim)
    tile_rows = lat_cells // TS
    tile_cols = lon_cells // TS
    tile_total = tile_rows * tile_cols
    lon_devices = lax.axis_size("lon")
    capacity = max(2, 7 * tile_total // (4 * lon_devices))
    slot_total = capacity * lon_devices
    lat_basis = basis_lat.reshape(SUB, tile_rows, TS)
    partial_value = jnp.einsum(
        "sja,jac->sjc", lat_basis, height.reshape(tile_rows, TS, lon_cells), precision=highest
    )
    product = partial_value * basis_lon[:, None, :]
    sensitivity = jnp.sum(product.reshape(SUB, tile_rows, tile_cols, TS), axis=3).reshape(
        SUB, tile_total
    )
    active = (jnp.arange(SUB)[:, None] < tile_count.reshape(1, tile_total)).astype(jnp.float32)
    sensitivity = sensitivity * active
    owners = tile_owner.reshape(tile_total)
    patches = tile_patch.reshape(tile_total)
    owner_hot = (owners[:, None] == jnp.arange(lon_devices)[None, :]).astype(jnp.float32)
    earlier = (jnp.arange(tile_total)[:, None] > jnp.arange(tile_total)[None, :]).astype(
        jnp.float32
    )
    before = jnp.dot(earlier, owner_hot, precision=highest)
    rank_within = jnp.sum(before * owner_hot, axis=1).astype(jnp.int32)
    slot_index = owners * capacity + rank_within
    placing_mask = slot_index[:, None] == jnp.arange(slot_total)[None, :]
    placing = placing_mask.astype(jnp.float32)
    sent_values = jnp.dot(sensitivity, placing, precision=highest)
    sent_patches = jnp.sum(jnp.where(placing_mask, patches[:, None], 0), axis=0).reshape(
        1, slot_total
    )
    received, received_patches = (
        lax.all_to_all(sent_values, "lon", split_axis=1, concat_axis=1, tiled=True),
        lax.all_to_all(sent_patches, "lon", split_axis=1, concat_axis=1, tiled=True),
    )
    member = (received_patches.reshape(slot_total)[:, None] == jnp.arange(NPATCH)[None, :]).astype(
        jnp.float32
    )
    gathered = jnp.dot(received, member, precision=highest)
    covariance = prior_patches.reshape(NPATCH, NPATCH)
    mixed = jnp.einsum("sn,mn->sm", gathered, covariance, precision=highest)
    smoothed = jnp.einsum("st,sm->tm", prior_subfaults, mixed, precision=highest)
    replies = jnp.einsum("tm,km->tk", smoothed, member, precision=highest)
    returned = lax.all_to_all(replies, "lon", split_axis=1, concat_axis=1, tiled=True)
    tile_value = jnp.einsum("sk,tk->st", returned, placing, precision=highest) * active
    spread_value = tile_value.reshape(SUB, tile_rows, tile_cols, 1) * basis_lon.reshape(
        SUB, 1, tile_cols, TS
    )
    weighted = spread_value.reshape(SUB, tile_rows, lon_cells)
    gradient = jnp.einsum("sja,sjc->jac", lat_basis, weighted, precision=highest).reshape(
        lat_cells, lon_cells
    )
    return (height, gradient)


def solution(mesh):
    return jax.shard_map(
        local,
        mesh=mesh,
        in_specs=(
            P("lat", "lon"),
            P("lat", "lon"),
            P("lat", "lon"),
            P(None, "lat"),
            P(None, "lon"),
            P("lat", "lon"),
            P("lat", "lon"),
            P("lat", "lon"),
            P("lat", "lon", None, None),
            P(),
        ),
        out_specs=(P("lat", "lon"), P("lat", "lon")),
        check_vma=False,
    )
```

profile of v0, /device:TPU:0, one launch (start us, length us, event | category | flops | bytes accessed | tf_op | source)
XLA Modules:
  0.0 121.1 jit_solution(4887672912142463356)
XLA Ops:
  0.7 1.1 multiply_bitcast_fusion
  1.8 1.2 %slice_maximum_fusion = (f32[2,512,1]{2,1,0:T(8,128)S(1)}, f32[2,512,1]{2,1,0:T(8,128)S(1)}) fusion(f32[1,512,128]{2,1,0:T(8,128)S(1)} %multiply_bitcast_fusion, f32[1,512,128]{2,1,0:T(8,128)} %bitcast.85), kind=kLoop, calls=%fused_computation.99 | loop fusion | flops 2048 | bytes 532480 | tf_op jit(solution)/shard_map/stack | solution.py:65
  3.0 4.5 %collective-permute-start.1 = (f32[2,512,1]{2,1,0:T(8,128)S(1)}, f32[2,512,1]{2,1,0:T(8,128)S(1)}, u32[]{:S(2)}, u32[]{:S(2)}) collective-permute-start(f32[2,512,1]{2,1,0:T(8,128)S(1)} %get-tuple-element.42), channel_id=1, source_target_pairs={{4,0},{8,4},{12,8},{16,12},{20,16},{24,20},{28,24},{0,28},{5,1},{9... | collective-permute-start | bytes 12296 | tf_op jit(solution)/shard_map/ppermute | solution.py:25
  7.5 10.4 %collective-permute-done.1 = f32[2,512,1]{2,1,0:T(8,128)S(1)} collective-permute-done((f32[2,512,1]{2,1,0:T(8,128)S(1)}, f32[2,512,1]{2,1,0:T(8,128)S(1)}, u32[]{:S(2)}, u32[]{:S(2)}) %collective-permute-start.1) | collective-permute-done | bytes 4128 | tf_op jit(solution)/shard_map/ppermute | solution.py:25
  17.9 2.9 %collective-permute-done = f32[2,512,1]{2,1,0:T(8,128)S(1)} collective-permute-done((f32[2,512,1]{2,1,0:T(8,128)S(1)}, f32[2,512,1]{2,1,0:T(8,128)S(1)}, u32[]{:S(2)}, u32[]{:S(2)}) %collective-permute-start) | collective-permute-done | bytes 4128 | tf_op jit(solution)/shard_map/ppermute | solution.py:22
  21.0 1.3 %collective-permute-start.3 = (f32[2,1,130]{2,1,0:T(1,128)S(1)}, f32[2,1,130]{2,1,0:T(1,128)S(1)}, u32[]{:S(2)}, u32[]{:S(2)}) collective-permute-start(f32[2,1,130]{2,1,0:T(1,128)S(1)} %get-tuple-element.22), channel_id=1, source_target_pairs={{1,0},{2,1},{3,2},{5,4},{6,5},{7,6},{9,8},{10,9},{11,10},{13,12},{... | collective-permute-start | bytes 3128 | tf_op jit(solution)/shard_map/ppermute | solution.py:25
  22.3 4.5 %collective-permute-start.2 = (f32[2,1,130]{2,1,0:T(1,128)S(1)}, f32[2,1,130]{2,1,0:T(1,128)S(1)}, u32[]{:S(2)}, u32[]{:S(2)}) collective-permute-start(f32[2,1,130]{2,1,0:T(1,128)S(1)} %get-tuple-element.23), channel_id=1, source_target_pairs={{0,1},{1,2},{2,3},{4,5},{5,6},{6,7},{8,9},{9,10},{10,11},{12,13},{... | collective-permute-start | bytes 3128 | tf_op jit(solution)/shard_map/ppermute | solution.py:22
  26.8 1.3 %collective-permute-done.2 = f32[2,1,130]{2,1,0:T(1,128)S(1)} collective-permute-done((f32[2,1,130]{2,1,0:T(1,128)S(1)}, f32[2,1,130]{2,1,0:T(1,128)S(1)}, u32[]{:S(2)}, u32[]{:S(2)}) %collective-permute-start.2) | collective-permute-done | bytes 1072 | tf_op jit(solution)/shard_map/ppermute | solution.py:22
  28.7 0.9 pad_maximum_fusion.1
  33.1 3.5 %collective-permute-done.4 = f32[3,512,1]{1,2,0:T(1,128)S(1)} collective-permute-done((f32[3,512,1]{1,2,0:T(1,128)S(1)}, f32[3,512,1]{1,2,0:T(1,128)S(1)}, u32[]{:S(2)}, u32[]{:S(2)}) %collective-permute-start.4) | collective-permute-done | bytes 6176 | tf_op jit(solution)/shard_map/ppermute | solution.py:22
  36.9 0.8 pad_maximum_fusion.64
  37.7 4.3 %collective-permute-start.6 = (f32[3,1,130]{2,1,0:T(1,128)S(1)}, f32[3,1,130]{2,1,0:T(1,128)S(1)}, u32[]{:S(2)}, u32[]{:S(2)}) collective-permute-start(f32[3,1,130]{2,1,0:T(1,128)S(1)} %get-tuple-element.19), channel_id=1, source_target_pairs={{0,1},{1,2},{2,3},{4,5},{5,6},{6,7},{8,9},{9,10},{10,11},{12,13},{... | collective-permute-start | bytes 4688 | tf_op jit(solution)/shard_map/ppermute | solution.py:22
  42.0 1.3 %collective-permute-start.7 = (f32[3,1,130]{2,1,0:T(1,128)S(1)}, f32[3,1,130]{2,1,0:T(1,128)S(1)}, u32[]{:S(2)}, u32[]{:S(2)}) collective-permute-start(f32[3,1,130]{2,1,0:T(1,128)S(1)} %get-tuple-element.18), channel_id=1, source_target_pairs={{1,0},{2,1},{3,2},{5,4},{6,5},{7,6},{9,8},{10,9},{11,10},{13,12},{... | collective-permute-start | bytes 4688 | tf_op jit(solution)/shard_map/ppermute | solution.py:25
  43.5 5.2 %collective-permute-done.7 = f32[3,1,130]{2,1,0:T(1,128)S(1)} collective-permute-done((f32[3,1,130]{2,1,0:T(1,128)S(1)}, f32[3,1,130]{2,1,0:T(1,128)S(1)}, u32[]{:S(2)}, u32[]{:S(2)}) %collective-permute-start.7) | collective-permute-done | bytes 1592 | tf_op jit(solution)/shard_map/ppermute | solution.py:25
  53.8 3.5 %collective-permute-done.8 = f32[3,512,1]{1,2,0:T(1,128)S(1)} collective-permute-done((f32[3,512,1]{1,2,0:T(1,128)S(1)}, f32[3,512,1]{1,2,0:T(1,128)S(1)}, u32[]{:S(2)}, u32[]{:S(2)}) %collective-permute-start.8) | collective-permute-done | bytes 6176 | tf_op jit(solution)/shard_map/ppermute | solution.py:22
  57.6 0.8 pad_maximum_fusion.59
  58.4 4.8 %collective-permute-start.10 = (f32[3,1,130]{2,1,0:T(1,128)S(1)}, f32[3,1,130]{2,1,0:T(1,128)S(1)}, u32[]{:S(2)}, u32[]{:S(2)}) collective-permute-start(f32[3,1,130]{2,1,0:T(1,128)S(1)} %get-tuple-element.17), channel_id=1, source_target_pairs={{0,1},{1,2},{2,3},{4,5},{5,6},{6,7},{8,9},{9,10},{10,11},{12,13},{... | collective-permute-start | bytes 4688 | tf_op jit(solution)/shard_map/ppermute | solution.py:22
  63.2 1.3 %collective-permute-start.11 = (f32[3,1,130]{2,1,0:T(1,128)S(1)}, f32[3,1,130]{2,1,0:T(1,128)S(1)}, u32[]{:S(2)}, u32[]{:S(2)}) collective-permute-start(f32[3,1,130]{2,1,0:T(1,128)S(1)} %get-tuple-element.16), channel_id=1, source_target_pairs={{1,0},{2,1},{3,2},{5,4},{6,5},{7,6},{9,8},{10,9},{11,10},{13,12},{... | collective-permute-start | bytes 4688 | tf_op jit(solution)/shard_map/ppermute | solution.py:25
  64.7 4.0 %collective-permute-done.11 = f32[3,1,130]{2,1,0:T(1,128)S(1)} collective-permute-done((f32[3,1,130]{2,1,0:T(1,128)S(1)}, f32[3,1,130]{2,1,0:T(1,128)S(1)}, u32[]{:S(2)}, u32[]{:S(2)}) %collective-permute-start.11) | collective-permute-done | bytes 1592 | tf_op jit(solution)/shard_map/ppermute | solution.py:25
  73.8 4.3 %all-to-all-start.1 = ((s32[1,8,56]{2,0,1:T(1,128)}), s32[1,8,56]{2,0,1:T(1,128)S(1)}, u32[]{:S(2)}, u32[]{:S(2)}) async-start(s32[1,8,56]{2,0,1:T(1,128)} %all_to_all.22), calls=%async_computation.1 | async-start | bytes 8192 | tf_op jit(solution)/shard_map/all_to_all | solution.py:105
  78.7 0.8 pad_maximum_fusion.54
  79.6 2.8 %collective-permute-start.14 = (f32[3,1,130]{2,1,0:T(1,128)S(1)}, f32[3,1,130]{2,1,0:T(1,128)S(1)}, u32[]{:S(2)}, u32[]{:S(2)}) collective-permute-start(f32[3,1,130]{2,1,0:T(1,128)S(1)} %get-tuple-element.15), channel_id=1, source_target_pairs={{0,1},{1,2},{2,3},{4,5},{5,6},{6,7},{8,9},{9,10},{10,11},{12,13},{... | collective-permute-start | bytes 4688 | tf_op jit(solution)/shard_map/ppermute | solution.py:22
  82.4 1.5 %collective-permute-start.15 = (f32[3,1,130]{2,1,0:T(1,128)S(1)}, f32[3,1,130]{2,1,0:T(1,128)S(1)}, u32[]{:S(2)}, u32[]{:S(2)}) collective-permute-start(f32[3,1,130]{2,1,0:T(1,128)S(1)} %get-tuple-element.14), channel_id=1, source_target_pairs={{1,0},{2,1},{3,2},{5,4},{6,5},{7,6},{9,8},{10,9},{11,10},{13,12},{... | collective-permute-start | bytes 4688 | tf_op jit(solution)/shard_map/ppermute | solution.py:25
  83.9 0.8 copy.80
  84.9 3.0 %collective-permute-done.15 = f32[3,1,130]{2,1,0:T(1,128)S(1)} collective-permute-done((f32[3,1,130]{2,1,0:T(1,128)S(1)}, f32[3,1,130]{2,1,0:T(1,128)S(1)}, u32[]{:S(2)}, u32[]{:S(2)}) %collective-permute-start.15) | collective-permute-done | bytes 1592 | tf_op jit(solution)/shard_map/ppermute | solution.py:25
  91.1 1.0 fusion
  94.1 0.8 reshape.136
  94.8 5.1 %all-to-all-start = ((f32[8,1,1792]{2,1,0:T(1,128)}), f32[8,1,1792]{2,1,0:T(1,128)S(1)}, u32[]{:S(2)}, u32[]{:S(2)}) async-start(f32[8,1,1792]{2,1,0:T(1,128)} %reshape.136), calls=%async_computation | async-start | bytes 114688 | tf_op jit(solution)/shard_map/all_to_all | solution.py:104
  101.3 4.5 %all-to-all-done = f32[8,1,1792]{2,1,0:T(1,128)S(1)} async-done(((f32[8,1,1792]{2,1,0:T(1,128)}), f32[8,1,1792]{2,1,0:T(1,128)S(1)}, u32[]{:S(2)}, u32[]{:S(2)}) %all-to-all-start) | async-done | bytes 57376 | tf_op jit(solution)/shard_map/all_to_all | solution.py:104
  109.1 8.2 %all_to_all.30 = f32[8,1,1792]{2,1,0:T(1,128)S(1)} all-to-all(f32[8,1,1792]{2,1,0:T(1,128)S(1)} %reshape.138), channel_id=1, replica_groups=mesh['lon'=8,'lat'=4] {'lon'}, dimensions={0} | all-to-all | bytes 114688 | tf_op jit(solution)/shard_map/all_to_all | solution.py:115
  117.3 0.8 reduce.5
  119.8 1.3 %fusion.28 = f32[32,128,16]{1,2,0:T(8,128)} fusion(f32[32,32,16]{0,2,1:T(8,128)S(1)} %bitcast.90, f32[32,32,128]{2,0,1:T(8,128)S(1)} %copy.91, f32[32,128]{1,0:T(8,128)S(1)} %copy-done.10), kind=kOutput, calls=%fused_computation.100 | convolution fusion | flops 25296896 | bytes 868352 | tf_op jit(solution)/shard_map/sja,sjc->jac/dot_general | solution.py:121
  (123 shorter events, 27.1 us)
Async XLA Ops:
  0.6 107.1 %copy-start = (f32[1,1,256,256]{3,2,1,0:T(8,128)S(1)}, f32[1,1,256,256]{3,2,1,0:T(8,128)}, u32[]{:S(2)}) copy-start(f32[1,1,256,256]{3,2,1,0:T(8,128)} %param.18) | copy-start | bytes 786436
  0.6 20.2 %copy-start.7 = (f32[512,128]{1,0:T(8,128)S(1)}, f32[512,128]{1,0:T(8,128)}, u32[]{:S(2)}) copy-start(f32[512,128]{1,0:T(8,128)} %param.10) | copy-start | bytes 786436
  3.0 14.9 %collective-permute-start.1 = (f32[2,512,1]{2,1,0:T(8,128)S(1)}, f32[2,512,1]{2,1,0:T(8,128)S(1)}, u32[]{:S(2)}, u32[]{:S(2)}) collective-permute-start(f32[2,512,1]{2,1,0:T(8,128)S(1)} %get-tuple-element.42), channel_id=1, source_target_pairs={{4,0},{8,4},{12,8},{16,12},{20,16},{24,20},{28,24},{0,28},{5,1},{9... | collective-permute-start | bytes 12296 | tf_op jit(solution)/shard_map/ppermute | solution.py:25
  7.5 13.3 %collective-permute-start = (f32[2,512,1]{2,1,0:T(8,128)S(1)}, f32[2,512,1]{2,1,0:T(8,128)S(1)}, u32[]{:S(2)}, u32[]{:S(2)}) collective-permute-start(f32[2,512,1]{2,1,0:T(8,128)S(1)} %get-tuple-element.41), channel_id=1, source_target_pairs={{0,4},{4,8},{8,12},{12,16},{16,20},{20,24},{24,28},{28,0},{1,5},{5... | collective-permute-start | bytes 12296 | tf_op jit(solution)/shard_map/ppermute | solution.py:22
  21.0 5.9 %collective-permute-start.3 = (f32[2,1,130]{2,1,0:T(1,128)S(1)}, f32[2,1,130]{2,1,0:T(1,128)S(1)}, u32[]{:S(2)}, u32[]{:S(2)}) collective-permute-start(f32[2,1,130]{2,1,0:T(1,128)S(1)} %get-tuple-element.22), channel_id=1, source_target_pairs={{1,0},{2,1},{3,2},{5,4},{6,5},{7,6},{9,8},{10,9},{11,10},{13,12},{... | collective-permute-start | bytes 3128 | tf_op jit(solution)/shard_map/ppermute | solution.py:25
  22.3 5.8 %collective-permute-start.2 = (f32[2,1,130]{2,1,0:T(1,128)S(1)}, f32[2,1,130]{2,1,0:T(1,128)S(1)}, u32[]{:S(2)}, u32[]{:S(2)}) collective-permute-start(f32[2,1,130]{2,1,0:T(1,128)S(1)} %get-tuple-element.23), channel_id=1, source_target_pairs={{0,1},{1,2},{2,3},{4,5},{5,6},{6,7},{8,9},{9,10},{10,11},{12,13},{... | collective-permute-start | bytes 3128 | tf_op jit(solution)/shard_map/ppermute | solution.py:22
  31.4 1.4 %collective-permute-start.5 = (f32[3,512,1]{1,2,0:T(1,128)S(1)}, f32[3,512,1]{1,2,0:T(1,128)S(1)}, u32[]{:S(2)}, u32[]{:S(2)}) collective-permute-start(f32[3,512,1]{1,2,0:T(1,128)S(1)} %copy.68), channel_id=1, source_target_pairs={{4,0},{8,4},{12,8},{16,12},{20,16},{24,20},{28,24},{0,28},{5,1},{9... | collective-permute-start | bytes 18440 | tf_op jit(solution)/shard_map/ppermute | solution.py:25
  31.7 4.9 %collective-permute-start.4 = (f32[3,512,1]{1,2,0:T(1,128)S(1)}, f32[3,512,1]{1,2,0:T(1,128)S(1)}, u32[]{:S(2)}, u32[]{:S(2)}) collective-permute-start(f32[3,512,1]{1,2,0:T(1,128)S(1)} %copy.67), channel_id=1, source_target_pairs={{0,4},{4,8},{8,12},{12,16},{16,20},{20,24},{24,28},{28,0},{1,5},{5... | collective-permute-start | bytes 18440 | tf_op jit(solution)/shard_map/ppermute | solution.py:22
  36.9 6.4 %copy-start.13 = (s32[32,8]{0,1:T(8,128)S(1)}, s32[32,8]{0,1:T(8,128)}, u32[]{:S(2)}) copy-start(s32[32,8]{0,1:T(8,128)} %param.15) | copy-start | bytes 3076
  37.7 5.8 %collective-permute-start.6 = (f32[3,1,130]{2,1,0:T(1,128)S(1)}, f32[3,1,130]{2,1,0:T(1,128)S(1)}, u32[]{:S(2)}, u32[]{:S(2)}) collective-permute-start(f32[3,1,130]{2,1,0:T(1,128)S(1)} %get-tuple-element.19), channel_id=1, source_target_pairs={{0,1},{1,2},{2,3},{4,5},{5,6},{6,7},{8,9},{9,10},{10,11},{12,13},{... | collective-permute-start | bytes 4688 | tf_op jit(solution)/shard_map/ppermute | solution.py:22
  42.0 6.7 %collective-permute-start.7 = (f32[3,1,130]{2,1,0:T(1,128)S(1)}, f32[3,1,130]{2,1,0:T(1,128)S(1)}, u32[]{:S(2)}, u32[]{:S(2)}) collective-permute-start(f32[3,1,130]{2,1,0:T(1,128)S(1)} %get-tuple-element.18), channel_id=1, source_target_pairs={{1,0},{2,1},{3,2},{5,4},{6,5},{7,6},{9,8},{10,9},{11,10},{13,12},{... | collective-permute-start | bytes 4688 | tf_op jit(solution)/shard_map/ppermute | solution.py:25
  49.1 1.0 copy-start.6
  52.1 1.4 %collective-permute-start.9 = (f32[3,512,1]{1,2,0:T(1,128)S(1)}, f32[3,512,1]{1,2,0:T(1,128)S(1)}, u32[]{:S(2)}, u32[]{:S(2)}) collective-permute-start(f32[3,512,1]{1,2,0:T(1,128)S(1)} %copy.72), channel_id=1, source_target_pairs={{4,0},{8,4},{12,8},{16,12},{20,16},{24,20},{28,24},{0,28},{5,1},{9... | collective-permute-start | bytes 18440 | tf_op jit(solution)/shard_map/ppermute | solution.py:25
  52.4 4.9 %collective-permute-start.8 = (f32[3,512,1]{1,2,0:T(1,128)S(1)}, f32[3,512,1]{1,2,0:T(1,128)S(1)}, u32[]{:S(2)}, u32[]{:S(2)}) collective-permute-start(f32[3,512,1]{1,2,0:T(1,128)S(1)} %copy.71), channel_id=1, source_target_pairs={{0,4},{4,8},{8,12},{12,16},{16,20},{20,24},{24,28},{28,0},{1,5},{5... | collective-permute-start | bytes 18440 | tf_op jit(solution)/shard_map/ppermute | solution.py:22
  57.6 7.0 %copy-start.14 = (s32[32,8]{0,1:T(8,128)S(1)}, s32[32,8]{0,1:T(8,128)}, u32[]{:S(2)}) copy-start(s32[32,8]{0,1:T(8,128)} %param.16) | copy-start | bytes 3076
  58.4 6.3 %collective-permute-start.10 = (f32[3,1,130]{2,1,0:T(1,128)S(1)}, f32[3,1,130]{2,1,0:T(1,128)S(1)}, u32[]{:S(2)}, u32[]{:S(2)}) collective-permute-start(f32[3,1,130]{2,1,0:T(1,128)S(1)} %get-tuple-element.17), channel_id=1, source_target_pairs={{0,1},{1,2},{2,3},{4,5},{5,6},{6,7},{8,9},{9,10},{10,11},{12,13},{... | collective-permute-start | bytes 4688 | tf_op jit(solution)/shard_map/ppermute | solution.py:22
  63.2 5.5 %collective-permute-start.11 = (f32[3,1,130]{2,1,0:T(1,128)S(1)}, f32[3,1,130]{2,1,0:T(1,128)S(1)}, u32[]{:S(2)}, u32[]{:S(2)}) collective-permute-start(f32[3,1,130]{2,1,0:T(1,128)S(1)} %get-tuple-element.16), channel_id=1, source_target_pairs={{1,0},{2,1},{3,2},{5,4},{6,5},{7,6},{9,8},{10,9},{11,10},{13,12},{... | collective-permute-start | bytes 4688 | tf_op jit(solution)/shard_map/ppermute | solution.py:25
  69.2 1.0 copy-start.4
  71.2 0.7 copy-start.1
  72.1 6.0 %collective-permute-start.13 = (f32[3,512,1]{1,2,0:T(1,128)S(1)}, f32[3,512,1]{1,2,0:T(1,128)S(1)}, u32[]{:S(2)}, u32[]{:S(2)}) collective-permute-start(f32[3,512,1]{1,2,0:T(1,128)S(1)} %copy.76), channel_id=1, source_target_pairs={{4,0},{8,4},{12,8},{16,12},{20,16},{24,20},{28,24},{0,28},{5,1},{9... | collective-permute-start | bytes 18440 | tf_op jit(solution)/shard_map/ppermute | solution.py:25
  72.4 6.0 %collective-permute-start.12 = (f32[3,512,1]{1,2,0:T(1,128)S(1)}, f32[3,512,1]{1,2,0:T(1,128)S(1)}, u32[]{:S(2)}, u32[]{:S(2)}) collective-permute-start(f32[3,512,1]{1,2,0:T(1,128)S(1)} %copy.75), channel_id=1, source_target_pairs={{0,4},{4,8},{8,12},{12,16},{16,20},{20,24},{24,28},{28,0},{1,5},{5... | collective-permute-start | bytes 18440 | tf_op jit(solution)/shard_map/ppermute | solution.py:22
  73.8 21.1 %all-to-all-start.1 = ((s32[1,8,56]{2,0,1:T(1,128)}), s32[1,8,56]{2,0,1:T(1,128)S(1)}, u32[]{:S(2)}, u32[]{:S(2)}) async-start(s32[1,8,56]{2,0,1:T(1,128)} %all_to_all.22), calls=%async_computation.1 | async-start | bytes 8192 | tf_op jit(solution)/shard_map/all_to_all | solution.py:105
  78.7 5.2 %copy-start.11 = (f32[32,512]{1,0:T(8,128)S(1)}, f32[32,512]{1,0:T(8,128)}, u32[]{:S(2)}) copy-start(f32[32,512]{1,0:T(8,128)} %param.13) | copy-start | bytes 196612
  78.7 6.0 %copy-start.15 = (s32[32,8]{0,1:T(8,128)S(1)}, s32[32,8]{0,1:T(8,128)}, u32[]{:S(2)}) copy-start(s32[32,8]{0,1:T(8,128)} %param.17) | copy-start | bytes 3076
  79.6 5.3 %collective-permute-start.14 = (f32[3,1,130]{2,1,0:T(1,128)S(1)}, f32[3,1,130]{2,1,0:T(1,128)S(1)}, u32[]{:S(2)}, u32[]{:S(2)}) collective-permute-start(f32[3,1,130]{2,1,0:T(1,128)S(1)} %get-tuple-element.15), channel_id=1, source_target_pairs={{0,1},{1,2},{2,3},{4,5},{5,6},{6,7},{8,9},{9,10},{10,11},{12,13},{... | collective-permute-start | bytes 4688 | tf_op jit(solution)/shard_map/ppermute | solution.py:22
  82.4 5.5 %collective-permute-start.15 = (f32[3,1,130]{2,1,0:T(1,128)S(1)}, f32[3,1,130]{2,1,0:T(1,128)S(1)}, u32[]{:S(2)}, u32[]{:S(2)}) collective-permute-start(f32[3,1,130]{2,1,0:T(1,128)S(1)} %get-tuple-element.14), channel_id=1, source_target_pairs={{1,0},{2,1},{3,2},{5,4},{6,5},{7,6},{9,8},{10,9},{11,10},{13,12},{... | collective-permute-start | bytes 4688 | tf_op jit(solution)/shard_map/ppermute | solution.py:25
  88.4 1.0 copy-start.2
  90.0 1.1 copy-start.8
  90.0 1.1 copy-start.10
  90.4 0.7 copy-start.9
  93.3 14.8 %copy-start.12 = (f32[32,32]{1,0:T(8,128)S(1)}, f32[32,32]{1,0:T(8,128)}, u32[]{:S(2)}) copy-start(f32[32,32]{1,0:T(8,128)} %param.19) | copy-start | bytes 12292
  94.8 11.0 %all-to-all-start = ((f32[8,1,1792]{2,1,0:T(1,128)}), f32[8,1,1792]{2,1,0:T(1,128)S(1)}, u32[]{:S(2)}, u32[]{:S(2)}) async-start(f32[8,1,1792]{2,1,0:T(1,128)} %reshape.136), calls=%async_computation | async-start | bytes 114688 | tf_op jit(solution)/shard_map/all_to_all | solution.py:104
  (2 other events, 1.4 us)
where the time goes:
time: 122 us; the launch traced here: 121 us
  waiting for transfers between devices  39.2 us (32%)
  starting transfers between devices  37.4 us (31%)
  other arithmetic  15.3 us (13%)
  local copies, waits for them, and re-layouts  15 us (12%)
  blocking collectives  8.25 us (7%)
  matrix products  4.59 us (4%)
  between operations  1.38 us (1%)
    ppermute x8, waiting for transfers between devices, padded(): lax.ppermute(lax.slice_in_dim(block, 0, width, axis=dim), axis, backward)  23.5 us
    ppermute x8, starting transfers between devices, padded(): lax.ppermute(lax.slice_in_dim(block, block.shape[dim] - width, None, axis...  18 us
    ppermute x8, waiting for transfers between devices, padded(): lax.ppermute(lax.slice_in_dim(block, block.shape[dim] - width, None, axis...  11.2 us
    ppermute x8, starting transfers between devices, padded(): lax.ppermute(lax.slice_in_dim(block, 0, width, axis=dim), axis, backward)  9.97 us
    all_to_all x1, blocking collectives, local(): lax.all_to_all(replies, 'lon', split_axis=1, concat_axis=1, tiled=True)  8.25 us
    unnamed x40, local copies, waits for them, and re-layouts  6.29 us
    all_to_all x1, starting transfers between devices, local(): lax.all_to_all(sent_values, 'lon', split_axis=1, concat_axis=1, tiled=True)  5.1 us
    all_to_all x1, waiting for transfers between devices, local(): lax.all_to_all(sent_values, 'lon', split_axis=1, concat_axis=1, tiled=True)  4.53 us
  transfers between devices with their start and end apart: 18, of which 11 were waited for; matrix products, arithmetic and copies ran while one was open for 9% of the time, Pallas kernels for 0%

commit v1 on v0

v1 whole, which is shorter than its diff:
```python
import functools

import jax
import jax.numpy as jnp
from jax import lax
from jax.experimental import pallas as pl
from jax.experimental.pallas import tpu as pltpu
from jax.sharding import PartitionSpec as P

STEPS = 4
TS = 16
SUB = 32
NPATCH = 256
COURANT = 0.6
GROUPS = 4
CHUNK = 32
MESH = pl.DeviceIdType.MESH

F32 = jnp.float32
BF16 = jnp.bfloat16


def iota(shape, dim):
    return lax.broadcasted_iota(jnp.int32, shape, dim)


def hot(mask):
    return jnp.where(mask, 1.0, 0.0).astype(BF16)


def split(x):
    high = x.astype(BF16)
    return high, (x - high.astype(F32)).astype(BF16)


def dot(a, b, contract=((1,), (0,))):
    return lax.dot_general(a, b, (contract, ((), ())), preferred_element_type=F32)


def select_dot(mask, x):
    width = x.shape[1]
    high, low = split(x)
    both = dot(mask, jnp.concatenate([high, low], axis=1))
    return both[:, :width] + both[:, width:]


def exact_dot(a, b, contract):
    return lax.dot_general(
        a, b, (contract, ((), ())), precision=lax.Precision.HIGHEST, preferred_element_type=F32
    )


def kernel(
    lon_count,
    lat_count,
    slot_rows,
    height_in,
    depth_in,
    wet_in,
    basis_lat,
    basis_lon,
    owner_in,
    patch_in,
    count_in,
    prior_patches,
    prior_subfaults,
    height_out,
    gradient_out,
    edge_send,
    edge_recv,
    side_send,
    side_recv,
    height_ext,
    depth_ext,
    patch_send,
    patch_recv,
    value_send,
    value_recv,
    reply_send,
    reply_recv,
    place,
    place_back,
    member,
    member_prior,
    halo_send_sem,
    halo_recv_sem,
    peer_send_sem,
    peer_recv_sem,
):
    lat = lax.axis_index("lat")
    lon = lax.axis_index("lon")
    rows, cols = height_in.shape
    tile_rows, tile_cols = rows // TS, cols // TS
    tiles = tile_rows * tile_cols
    block = lon_count * slot_rows
    slots = GROUPS * block
    up, down = lax.rem(lat + lat_count - 1, lat_count), lax.rem(lat + 1, lat_count)
    left, right = lax.rem(lon + lon_count - 1, lon_count), lax.rem(lon + 1, lon_count)

    def peer(offset):
        return lax.rem(lon + offset, lon_count)

    def each_peer(body):
        if lon_count <= 8:
            for offset in range(1, lon_count):
                body(offset)
        else:
            def step(offset, carry):
                body(offset)
                return carry

            lax.fori_loop(1, lon_count, step, 0)

    barrier = pltpu.get_barrier_semaphore()

    def greet(lat_at, lon_at):
        pl.semaphore_signal(barrier, inc=1, device_id=(lon_at, lat_at), device_id_type=MESH)

    each_peer(lambda offset: greet(lat, peer(offset)))
    for lat_at in (up, down):
        for lon_at in (left, lon, right):
            greet(lat_at, lon_at)

    wet_depth = depth_in[...] * wet_in[...].astype(F32)
    edge_send[0:8, :] = height_in[0:8, :]
    edge_send[8:16, :] = wet_depth[0:8, :]
    edge_send[16:24, :] = height_in[rows - 8 : rows, :]
    edge_send[24:32, :] = wet_depth[rows - 8 : rows, :]
    fields = jnp.concatenate([height_in[...], wet_depth], axis=1)
    pick_row, pick_col = iota((16, 2 * cols), 0), iota((16, 2 * cols), 1)
    pick_lane = pick_col % cols
    pick_field = pick_col // cols
    wanted = jnp.where(pick_row < 8, pick_row % 4, cols - 4 + pick_row % 4)
    pick = jnp.where((pick_lane == wanted) & (pick_field == (pick_row % 8) // 4), 1.0, 0.0)
    side_send[...] = exact_dot(pick, fields, ((1,), (1,)))

    pl.semaphore_wait(barrier, lon_count - 1 + 6)

    halo = []

    def send_halo(src, dst, lat_at, lon_at):
        index = len(halo)
        copy = pltpu.make_async_remote_copy(
            src_ref=src,
            dst_ref=dst,
            send_sem=halo_send_sem.at[index],
            recv_sem=halo_recv_sem.at[index],
            device_id=(lon_at, lat_at),
            device_id_type=MESH,
        )
        copy.start()
        halo.append(copy)

    send_halo(side_send.at[pl.ds(0, 8)], side_recv.at[pl.ds(0, 8)], lat, left)
    send_halo(side_send.at[pl.ds(8, 8)], side_recv.at[pl.ds(8, 8)], lat, right)
    for place_at, lon_at in ((0, lon), (1, left), (2, right)):
        send_halo(edge_send.at[pl.ds(0, 16)], edge_recv.at[place_at], up, lon_at)
    for place_at, lon_at in ((3, lon), (4, left), (5, right)):
        send_halo(edge_send.at[pl.ds(16, 16)], edge_recv.at[place_at], down, lon_at)

    def as_column(values):
        spread = dot(
            hot(iota((tiles, tile_rows), 0) % tile_rows == iota((tiles, tile_rows), 1)),
            values.astype(F32).astype(BF16),
        )
        keep = iota((tiles, tile_cols), 0) // tile_rows == iota((tiles, tile_cols), 1)
        return jnp.sum(jnp.where(keep, spread, 0.0), axis=1, keepdims=True)

    def as_row(values):
        spread = dot(
            values.astype(F32).astype(BF16),
            hot(iota((tile_cols, tiles), 1) // tile_rows == iota((tile_cols, tiles), 0)),
        )
        keep = iota((tile_rows, tiles), 1) % tile_rows == iota((tile_rows, tiles), 0)
        return jnp.sum(jnp.where(keep, spread, 0.0), axis=0, keepdims=True)

    owner_column, owner_row = as_column(owner_in[...]), as_row(owner_in[...])
    first, second = iota((tiles, tiles), 0), iota((tiles, tiles), 1)
    same = owner_column == owner_row
    rank_column = jnp.sum(jnp.where(same & (second < first), 1.0, 0.0), axis=1, keepdims=True)
    rank_row = jnp.sum(jnp.where(same & (first < second), 1.0, 0.0), axis=0, keepdims=True)

    def slot_of(owner, rank):
        owner, rank = owner.astype(jnp.int32), rank.astype(jnp.int32)
        return (rank // slot_rows) * block + owner * slot_rows + rank % slot_rows

    place[...] = hot(iota((slots, tiles), 0) == slot_of(owner_row, rank_row))
    patch_column = jnp.broadcast_to(as_column(patch_in[...]), (tiles, 128)).astype(BF16)
    sent_patch = dot(place[...], patch_column)
    patch_lane = iota((block, 128), 1)
    packed = jnp.zeros((block, 128), F32)
    for group in range(GROUPS):
        packed = jnp.where(patch_lane == group, sent_patch[group * block : (group + 1) * block], packed)
    patch_send[...] = packed

    def exchange(send, recv, phase):
        def descriptor(offset):
            target = peer(offset)
            return pltpu.make_async_remote_copy(
                src_ref=send.at[pl.ds(pl.multiple_of(target * slot_rows, 8), slot_rows)],
                dst_ref=recv.at[pl.ds(pl.multiple_of(lon * slot_rows, 8), slot_rows)],
                send_sem=peer_send_sem.at[phase, offset],
                recv_sem=peer_recv_sem.at[phase, offset],
                device_id=(target, lat),
                device_id_type=MESH,
            )

        each_peer(lambda offset: descriptor(offset).start())
        own = pl.ds(pl.multiple_of(lon * slot_rows, 8), slot_rows)
        recv[own, :] = send[own, :]
        return lambda: each_peer(lambda offset: descriptor(offset).wait())

    patches_done = exchange(patch_send, patch_recv, 0)
    place_back[...] = hot(iota((tiles, slots), 1) == slot_of(owner_column, rank_column))

    wide = tile_cols * SUB
    repeat_sub = jnp.where(iota((SUB, wide), 1) % SUB == iota((SUB, wide), 0), 1.0, 0.0)
    lat_wide = exact_dot(basis_lat[...], repeat_sub, ((0,), (0,)))
    lon_wide = exact_dot(basis_lon[...], repeat_sub, ((0,), (0,)))
    lon_wide = jnp.where(
        iota((cols, wide), 0) // TS == iota((cols, wide), 1) // SUB, lon_wide, 0.0
    )
    lon_high, lon_low = split(lon_wide)
    count_wide = dot(
        count_in[...].astype(F32).astype(BF16),
        hot(iota((tile_cols, wide), 1) // SUB == iota((tile_cols, wide), 0)),
    )
    active = jnp.where(
        (iota((tile_rows, wide), 1) % SUB).astype(F32) < count_wide, 1.0, 0.0
    )
    mixing = exact_dot(
        exact_dot(repeat_sub, prior_subfaults[...], ((0,), (0,))), repeat_sub, ((1,), (0,))
    )
    mixing = jnp.where(iota((wide, wide), 0) // SUB == iota((wide, wide), 1) // SUB, mixing, 0.0)
    mixing_high, mixing_low = split(mixing)

    for copy in halo:
        copy.wait()

    unpick_row, unpick_col = iota((16, 2 * cols), 0), iota((16, 2 * cols), 1)
    target = jnp.where(unpick_row < 8, unpick_row % 4, cols - 4 + unpick_row % 4)
    unpick = jnp.where(
        (unpick_col % cols == target) & (unpick_col // cols == (unpick_row % 8) // 4), 1.0, 0.0
    )
    sides = exact_dot(side_recv[...], unpick, ((0,), (0,)))
    edge_lane = iota((8, cols), 1)
    for at, ext, own in ((0, height_ext, height_in[...]), (8, depth_ext, wet_depth)):
        ext[4 : rows + 4, :cols] = own
        ext[4 : rows + 4, cols:] = sides[:, :cols] if at == 0 else sides[:, cols:]
        below = jnp.concatenate(
            [
                edge_recv[0, at : at + 8, :],
                jnp.where(edge_lane < cols // 2, edge_recv[1, at : at + 8, :], edge_recv[2, at : at + 8, :]),
            ],
            axis=1,
        )
        above = jnp.concatenate(
            [
                edge_recv[3, at : at + 8, :],
                jnp.where(edge_lane < cols // 2, edge_recv[4, at : at + 8, :], edge_recv[5, at : at + 8, :]),
            ],
            axis=1,
        )
        ext[0:4, :] = jnp.where(lat == 0, 0.0, above)[4:8]
        ext[rows + 4 : rows + 8, :] = jnp.where(lat == lat_count - 1, 0.0, below)[0:4]

    size = CHUNK + 8

    def stencil(chunk, carry):
        base = pl.ds(pl.multiple_of(chunk * CHUNK, 8), size)
        height, depth = height_ext[base, :], depth_ext[base, :]
        lanes = 2 * cols
        east_weight = COURANT * jnp.minimum(depth, pltpu.roll(depth, lanes - 1, 1))
        north_weight = COURANT * jnp.minimum(depth, pltpu.roll(depth, size - 1, 0))
        east = north = None
        for repeat in range(STEPS):
            east_add = east_weight * (pltpu.roll(height, lanes - 1, 1) - height)
            north_add = north_weight * (pltpu.roll(height, size - 1, 0) - height)
            east = east_add if repeat == 0 else east + east_add
            north = north_add if repeat == 0 else north + north_add
            height = (
                height
                + COURANT * (east - pltpu.roll(east, 1, 1))
                + COURANT * (north - pltpu.roll(north, 1, 0))
            )
        done = pltpu.roll(height[:, :cols], size - 4, 0)
        height_out[pl.ds(pl.multiple_of(chunk * CHUNK, 8), CHUNK), :] = done[:CHUNK]
        return carry

    lax.fori_loop(0, rows // CHUNK, stencil, 0)

    height_high, height_low = split(height_out[...])
    projected = dot(
        jnp.concatenate([height_high, height_low], axis=1),
        jnp.concatenate([lon_high, lon_high], axis=0),
    ) + dot(height_high, lon_low)
    sensitivity = jnp.sum((projected * lat_wide).reshape(tile_rows, TS, wide), axis=1) * active
    sense_high, sense_low = split(sensitivity)
    sensitivity = (
        dot(sense_high, mixing_high) + dot(sense_low, mixing_high) + dot(sense_high, mixing_low)
    )
    by_tile = jnp.concatenate(
        [sensitivity[:, c * SUB : (c + 1) * SUB] for c in range(tile_cols)], axis=0
    )

    def pack(x):
        return jnp.concatenate([x[g * block : (g + 1) * block] for g in range(GROUPS)], axis=1)

    def unpack(x):
        return jnp.concatenate([x[:, g * SUB : (g + 1) * SUB] for g in range(GROUPS)], axis=0)

    value_send[...] = pack(select_dot(place[...], by_tile))
    values_done = exchange(value_send, value_recv, 1)

    patches_done()
    patch_ids = patch_recv[...]
    patch_line = patch_ids.T
    for group in range(GROUPS):
        at = pl.ds(group * block, block)
        member[:, at] = hot(
            iota((NPATCH, block), 0).astype(F32) == patch_line[group : group + 1, :]
        )
        hit = hot(iota((block, NPATCH), 1).astype(F32) == patch_ids[:, group : group + 1])
        prior_high, prior_low = split(prior_patches[...])
        member_prior[at, :NPATCH] = dot(hit, prior_high).astype(BF16)
        member_prior[at, NPATCH:] = dot(hit, prior_low).astype(BF16)

    values_done()
    parameters = select_dot(member[...], unpack(value_recv[...]))
    par_high, par_low = split(parameters)
    both = dot(
        member_prior[...],
        jnp.concatenate(
            [
                jnp.concatenate([par_high, par_low], axis=1),
                jnp.concatenate([par_high, jnp.zeros_like(par_low)], axis=1),
            ],
            axis=0,
        ),
    )
    reply_send[...] = pack(both[:, :SUB] + both[:, SUB:])
    replies_done = exchange(reply_send, reply_recv, 2)
    replies_done()

    tile_value = select_dot(place_back[...], unpack(reply_recv[...]))
    tile_value = (
        jnp.concatenate(
            [tile_value[c * tile_rows : (c + 1) * tile_rows] for c in range(tile_cols)], axis=1
        )
        * active
    )
    spread = jnp.broadcast_to(tile_value[:, None, :], (tile_rows, TS, wide)).reshape(rows, wide)
    weighted_high, weighted_low = split(spread * lat_wide)
    contract = ((1,), (1,))
    gradient_out[...] = (
        dot(weighted_high, lon_high, contract)
        + dot(weighted_low, lon_high, contract)
        + dot(weighted_high, lon_low, contract)
    )


def local(
    lon_count,
    lat_count,
    adjoint_height,
    depth,
    wet,
    basis_lat,
    basis_lon,
    tile_owner,
    tile_patch,
    tile_count,
    prior_patches,
    prior_subfaults,
):
    rows, cols = adjoint_height.shape
    tiles = (rows // TS) * (cols // TS)
    capacity = max(2, 7 * tiles // (4 * lon_count))
    slot_rows = 8 * pl.cdiv(capacity, 8 * GROUPS)
    block = lon_count * slot_rows
    slots = GROUPS * block
    vmem = pl.BlockSpec(memory_space=pltpu.VMEM)
    packed = pltpu.VMEM((block, 128), F32)
    height, gradient = pl.pallas_call(
        functools.partial(kernel, lon_count, lat_count, slot_rows),
        out_shape=(
            jax.ShapeDtypeStruct((rows, cols), F32),
            jax.ShapeDtypeStruct((rows, cols), F32),
        ),
        in_specs=[vmem] * 10,
        out_specs=(vmem, vmem),
        scratch_shapes=[
            pltpu.VMEM((32, cols), F32),
            pltpu.VMEM((6, 16, cols), F32),
            pltpu.VMEM((16, rows), F32),
            pltpu.VMEM((16, rows), F32),
            pltpu.VMEM((rows + 8, 2 * cols), F32),
            pltpu.VMEM((rows + 8, 2 * cols), F32),
            packed,
            packed,
            packed,
            packed,
            packed,
            packed,
            pltpu.VMEM((slots, tiles), BF16),
            pltpu.VMEM((tiles, slots), BF16),
            pltpu.VMEM((NPATCH, slots), BF16),
            pltpu.VMEM((slots, 2 * NPATCH), BF16),
            pltpu.SemaphoreType.DMA((8,)),
            pltpu.SemaphoreType.DMA((8,)),
            pltpu.SemaphoreType.DMA((3, lon_count)),
            pltpu.SemaphoreType.DMA((3, lon_count)),
        ],
        compiler_params=pltpu.CompilerParams(
            collective_id=0, has_side_effects=True, vmem_limit_bytes=48 * 1024 * 1024
        ),
    )(
        adjoint_height,
        depth,
        wet,
        basis_lat,
        basis_lon,
        tile_owner,
        tile_patch,
        tile_count,
        prior_patches.reshape(NPATCH, NPATCH),
        prior_subfaults,
    )
    return height, gradient


def solution(mesh):
    return jax.shard_map(
        functools.partial(local, mesh.shape["lon"], mesh.shape["lat"]),
        mesh=mesh,
        in_specs=(
            P("lat", "lon"),
            P("lat", "lon"),
            P("lat", "lon"),
            P(None, "lat"),
            P(None, "lon"),
            P("lat", "lon"),
            P("lat", "lon"),
            P("lat", "lon"),
            P("lat", "lon", None, None),
            P(),
        ),
        out_specs=(P("lat", "lon"), P("lat", "lon")),
        check_vma=False,
    )
```

time: 122 us -> 40.8 us (0.33)
  waiting for transfers between devices: 39.2 us -> 0 us
  starting transfers between devices: 37.4 us -> 0 us
  Pallas kernels: 0 us -> 32.2 us
  other arithmetic: 15.3 us -> 0 us
  blocking collectives: 8.25 us -> 0 us
  local copies, waits for them, and re-layouts: 15 us -> 7.55 us
  matrix products: 4.59 us -> 0 us
    ppermute x16 -> x0, waiting for transfers between devices: 34.7 us -> none  [the longest x8 23.5 us: padded(): lax.ppermute(lax.slice_in_dim(block, 0, width, axis=dim), axis, backward)]
    pallas_call x0 -> x1, Pallas kernels: none -> 32.2 us  [local(): pl.pallas_call(functools.partial(kernel, lon_count, lat_count, slot_rows)...]
    ppermute x16 -> x0, starting transfers between devices: 28 us -> none  [the longest x8 18 us: padded(): lax.ppermute(lax.slice_in_dim(block, block.shape[dim] - width, None, axis...]
    all_to_all x2 -> x0, starting transfers between devices: 9.42 us -> none  [the longest x1 5.1 us: local(): lax.all_to_all(sent_values, 'lon', split_axis=1, concat_axis=1, tiled=True)]
    all_to_all x1 -> x0, blocking collectives: 8.25 us -> none  [local(): lax.all_to_all(replies, 'lon', split_axis=1, concat_axis=1, tiled=True)]
    dot_general x9 -> x0, matrix products: 4.59 us -> none  [the longest x1 1.31 us: local(): jnp.einsum('sja,sjc->jac', lat_basis, weighted, precision=highest)]
    all_to_all x2 -> x0, waiting for transfers between devices: 4.53 us -> none  [the longest x1 4.53 us: local(): lax.all_to_all(sent_values, 'lon', split_axis=1, concat_axis=1, tiled=True)]
    concatenate x6 -> x0, other arithmetic: 3.85 us -> none  [padded(): block = jnp.concatenate([low, block, high], axis=dim)]
  transfers between devices with their start and end apart: 18 -> 0, of which waited for: 11 -> 0; matrix products, arithmetic and copies ran while one was open for 9% -> 0% of each run, Pallas kernels for 0% -> 0%
where the time goes in v1:
time: 40.8 us; the launch traced here: 40.5 us
  Pallas kernels  32.2 us (79%)
  local copies, waits for them, and re-layouts  7.55 us (19%)
  between operations  0.67 us (2%)
    pallas_call x1, Pallas kernels, local(): pl.pallas_call(functools.partial(kernel, lon_count, lat_count, slot_rows)...  32.2 us
    unnamed x23, local copies, waits for them, and re-layouts  7.55 us

profile of v1, /device:TPU:0, one launch (start us, length us, event | category | flops | bytes accessed | tf_op | source)
XLA Modules:
  0.0 40.5 jit_solution(8120647894057255576)
XLA Ops:
  0.6 0.0 copy-start.7
  0.6 0.0 copy-start.8
  0.7 0.8 %copy.12.owner_in = s32[32,8]{1,0:T(8,128)S(1)} copy(s32[32,8]{0,1:T(8,128)} %param.15) | data formatting | bytes 2048 | tf_op args[5]
  1.4 0.0 copy-done.7
  1.4 0.0 copy-start.5
  1.4 0.0 copy-start.6
  1.4 0.1 copy.13.patch_in
  1.5 0.0 copy-done.8
  1.5 0.1 copy.14.count_in
  1.6 0.6 %copy-done.5 = f32[32,128]{1,0:T(8,128)S(1)} copy-done((f32[32,128]{1,0:T(8,128)S(1)}, f32[32,128]{1,0:T(8,128)}, u32[]{:S(2)}) %copy-start.5) | copy-done | bytes 16408
  2.1 0.0 copy-done.6
  2.2 0.0 copy-start
  2.2 0.9 %copy-done = f32[512,128]{1,0:T(8,128)S(1)} copy-done((f32[512,128]{1,0:T(8,128)S(1)}, f32[512,128]{1,0:T(8,128)}, u32[]{:S(2)}) %copy-start) | copy-done | bytes 262168
  3.1 0.0 copy-start.1
  3.1 0.9 %copy-done.1 = f32[512,128]{1,0:T(8,128)S(1)} copy-done((f32[512,128]{1,0:T(8,128)S(1)}, f32[512,128]{1,0:T(8,128)}, u32[]{:S(2)}) %copy-start.1) | copy-done | bytes 262168
  4.1 0.0 copy-start.2
  4.1 0.9 %copy-done.2 = s32[512,128]{1,0:T(8,128)S(1)} copy-done((s32[512,128]{1,0:T(8,128)S(1)}, s32[512,128]{1,0:T(8,128)}, u32[]{:S(2)}) %copy-start.2) | copy-done | bytes 262168
  5.0 0.0 copy-start.3
  5.0 0.9 %copy-done.3 = f32[1,1,256,256]{3,2,1,0:T(8,128)S(1)} copy-done((f32[1,1,256,256]{3,2,1,0:T(8,128)S(1)}, f32[1,1,256,256]{3,2,1,0:T(8,128)}, u32[]{:S(2)}) %copy-start.3) | copy-done | bytes 262168
  6.0 0.0 copy-start.4
  6.0 0.8 %copy-done.4 = f32[32,512]{1,0:T(8,128)S(1)} copy-done((f32[32,512]{1,0:T(8,128)S(1)}, f32[32,512]{1,0:T(8,128)}, u32[]{:S(2)}) %copy-start.4) | copy-done | bytes 65560
  6.8 32.2 %shard_map.113 = (f32[512,128]{1,0:T(8,128)S(1)}, f32[512,128]{1,0:T(8,128)S(1)}) custom-call(f32[512,128]{1,0:T(8,128)S(1)} %copy-done, f32[512,128]{1,0:T(8,128)S(1)} %copy-done.1, s32[512,128]{1,0:T(8,128)S(1)} %copy-done.2, f32[32,512]{1,0:T(8,128)S(1)} %copy-done.4, f32[32,128]{1,0:T(8,128)S(1)} %copy-done.5, s32[32,8]{1,0:T(8,128)S(1)} %copy.12.owner_in, ...), custom_call_target="tpu_custom_call" | custom-call | tf_op jit(solution)/shard_map/pallas_call | solution.py:384
  39.1 0.7 %copy.17 = f32[512,128]{1,0:T(8,128)} copy(f32[512,128]{1,0:T(8,128)S(1)} %get-tuple-element.4) | data formatting | bytes 524288
  39.8 0.7 %copy.18 = f32[512,128]{1,0:T(8,128)} copy(f32[512,128]{1,0:T(8,128)S(1)} %get-tuple-element.5) | data formatting | bytes 524288
Async XLA Ops:
  0.6 0.8 %copy-start.7 = (s32[32,8]{0,1:T(8,128)S(1)}, s32[32,8]{0,1:T(8,128)}, u32[]{:S(2)}) copy-start(s32[32,8]{0,1:T(8,128)} %param.16) | copy-start | bytes 3076
  0.6 0.9 %copy-start.8 = (s32[32,8]{0,1:T(8,128)S(1)}, s32[32,8]{0,1:T(8,128)}, u32[]{:S(2)}) copy-start(s32[32,8]{0,1:T(8,128)} %param.17) | copy-start | bytes 3076
  1.4 0.7 %copy-start.5 = (f32[32,128]{1,0:T(8,128)S(1)}, f32[32,128]{1,0:T(8,128)}, u32[]{:S(2)}) copy-start(f32[32,128]{1,0:T(8,128)} %basis_lon.1) | copy-start | bytes 49156
  1.4 0.7 %copy-start.6 = (f32[32,32]{1,0:T(8,128)S(1)}, f32[32,32]{1,0:T(8,128)}, u32[]{:S(2)}) copy-start(f32[32,32]{1,0:T(8,128)} %prior_subfaults.1) | copy-start | bytes 12292
  2.2 0.9 %copy-start = (f32[512,128]{1,0:T(8,128)S(1)}, f32[512,128]{1,0:T(8,128)}, u32[]{:S(2)}) copy-start(f32[512,128]{1,0:T(8,128)} %height_in.1) | copy-start | bytes 786436
  3.1 0.9 %copy-start.1 = (f32[512,128]{1,0:T(8,128)S(1)}, f32[512,128]{1,0:T(8,128)}, u32[]{:S(2)}) copy-start(f32[512,128]{1,0:T(8,128)} %depth_in.1) | copy-start | bytes 786436
  4.1 0.9 %copy-start.2 = (s32[512,128]{1,0:T(8,128)S(1)}, s32[512,128]{1,0:T(8,128)}, u32[]{:S(2)}) copy-start(s32[512,128]{1,0:T(8,128)} %wet_in.1) | copy-start | bytes 786436
  5.0 0.9 %copy-start.3 = (f32[1,1,256,256]{3,2,1,0:T(8,128)S(1)}, f32[1,1,256,256]{3,2,1,0:T(8,128)}, u32[]{:S(2)}) copy-start(f32[1,1,256,256]{3,2,1,0:T(8,128)} %param.18) | copy-start | bytes 786436
  6.0 0.8 %copy-start.4 = (f32[32,512]{1,0:T(8,128)S(1)}, f32[32,512]{1,0:T(8,128)}, u32[]{:S(2)}) copy-start(f32[32,512]{1,0:T(8,128)} %basis_lat.1) | copy-start | bytes 196612
